TPU v7x, 32 devices: a whole 2x2x4 slice. The times are simulated.
32 devices in a mesh: gx: 4 (over z), gy: 8 (over y, x, core).
Axes of the slice: x: 2, y: 2, z: 4, core: 2. Of those that a mesh axis runs over, the one named last changes fastest.
Arguments:
- image: float32 [64, 256, 256], P('gx', 'gy'), may hold values from -6 to 6
- phases: int32 [64, 256, 256], P('gx', 'gy'), may hold values from 0 to 2
- phase_table: float32 [2, 3], replicated, may hold values from 0.2 to 8
- start_potential: float32 [64, 256, 256], P('gx', 'gy'), may hold values from 0 to 1
Outputs:
- conductivity: float32 [64, 256, 256], P('gx', 'gy')
- potential: float32 [64, 256, 256], P('gx', 'gy')
Inputs may be any that keep to these rules, and one draw needn't show every extreme that they name: `phases`: 0 fibre, 1 binder, 2 pore.
All inputs are finite; a program needn't handle non-finite values.
Results may differ from a plain program's by a relative error of at most 0.00005.
Values sent between devices are 32-bit elements; how exact they have to be, the bound alone decides.
A program may use at most 128 MiB of HBM per device.

v0:
```python
import functools
import math

import jax
import jax.numpy as jnp
import ml_dtypes
import numpy as np
from jax import lax
from jax.experimental import pallas as pl
from jax.experimental.pallas import tpu as pltpu
from jax.sharding import PartitionSpec as P

SWEEPS = 3
PHASES = 3
DERIV = 3
SMOOTH = 12
IMG_X = DERIV + SMOOTH
IMG_Y = 16
POT_X = SWEEPS
POT_Y = 8
MESH = pl.DeviceIdType.MESH
VMEM_LIMIT = 58 * 1024 * 1024
F32 = jnp.float32
BF16 = jnp.bfloat16


def gauss_taps(sigma, reach, order):
    values = [math.exp(-t * t / (2.0 * sigma * sigma)) for t in range(-reach, reach + 1)]
    total = sum(values)
    values = [value / total for value in values]
    if order == 1:
        values = [(i - reach) * values[i] / (sigma * sigma) for i in range(2 * reach + 1)]
    return values


NEAR = gauss_taps(1.0, DERIV, 0)
SLOPE = gauss_taps(1.0, DERIV, 1)
WIDE = gauss_taps(4.0, SMOOTH, 0)


def halves(matrix):
    high = matrix.astype(ml_dtypes.bfloat16)
    low = (matrix - high.astype(np.float32)).astype(ml_dtypes.bfloat16)
    return high, low


def band(out_len, in_len, margin, taps, first=0, last=None):
    reach = (len(taps) - 1) // 2
    matrix = np.zeros((out_len, in_len), np.float32)
    for i in range(first, out_len if last is None else last):
        for t in range(-reach, reach + 1):
            k = i + margin + t
            if 0 <= k < in_len:
                matrix[i, k] = taps[t + reach]
    return matrix


def left_weights(matrix):
    high, low = halves(matrix)
    return np.concatenate([high, high, low], axis=1)


def right_weights(*matrices):
    parts = []
    for matrix in matrices:
        parts += list(halves(np.ascontiguousarray(matrix.T)))
    return np.concatenate(parts, axis=1)


def neighbours():
    gx, gy = lax.axis_index("gx"), lax.axis_index("gy")
    nx, ny = lax.axis_size("gx"), lax.axis_size("gy")
    has_x = (gx > 0, gx < nx - 1)
    has_y = (gy > 0, gy < ny - 1)
    at_x = ((gx - 1, gy), (gx + 1, gy))
    at_y = ((gx, gy - 1), (gx, gy + 1))
    return has_x, has_y, at_x, at_y


def greet():
    has_x, has_y, at_x, at_y = neighbours()
    barrier = pltpu.get_barrier_semaphore()
    for has, at in zip(has_x + has_y, at_x + at_y):
        @pl.when(has)
        def _(at=at):
            pl.semaphore_signal(barrier, inc=1, device_id=at, device_id_type=MESH)
    pl.semaphore_wait(barrier, sum(has.astype(jnp.int32) for has in has_x + has_y))


class Exchange:
    def __init__(self, own, ext, hx, hy, cuts, bands, send, recv):
        self.ext, self.hx, self.hy, self.cuts, self.bands = ext, hx, hy, cuts, bands
        self.send, self.recv = send, recv
        self.nx, self.ny = ext.shape[0] - 2 * hx, ext.shape[1] - 2 * hy
        self.own = own
        self.has_x, self.has_y, self.at_x, self.at_y = neighbours()

    @staticmethod
    def count(cuts, bands):
        return 2 * len(bands) + 6 * len(cuts)

    def remote(self, src, dst, index, at):
        return pltpu.make_async_remote_copy(
            src_ref=src, dst_ref=dst, send_sem=self.send.at[index],
            recv_sem=self.recv.at[index], device_id=at, device_id_type=MESH)

    def brick(self, row, rows, col, cols):
        if self.own is None:
            return self.ext.at[pl.ds(self.hx + row, rows), pl.ds(self.hy + col, cols)]
        return self.own.at[pl.ds(row, rows), pl.ds(col, cols)]

    def halo_rows(self, d, cut):
        a, b = cut
        if d == 0:
            return self.nx + self.hx + a, b - a
        return self.hx - b, b - a

    def copy_x(self, d, c):
        a, b = self.cuts[c]
        row, size = self.halo_rows(d, (a, b))
        start = a if d == 0 else self.nx - b
        return self.remote(
            self.brick(start, size, 0, self.ny),
            self.ext.at[pl.ds(row, size), pl.ds(self.hy, self.ny)],
            d * len(self.cuts) + c, self.at_x[d])

    def copy_y(self, d, k):
        a, b = self.bands[k]
        src = 0 if d == 0 else self.ny - self.hy
        dst = self.hy + self.ny if d == 0 else 0
        return self.remote(
            self.brick(a, b - a, src, self.hy),
            self.ext.at[pl.ds(self.hx + a, b - a), pl.ds(dst, self.hy)],
            6 * len(self.cuts) + d * len(self.bands) + k, self.at_y[d])

    def copy_corner(self, side, d, c):
        row, size = self.halo_rows(side, self.cuts[c])
        src = self.hy if d == 0 else self.ny
        dst = self.hy + self.ny if d == 0 else 0
        n = len(self.cuts)
        return self.remote(
            self.ext.at[pl.ds(row, size), pl.ds(src, self.hy)],
            self.ext.at[pl.ds(row, size), pl.ds(dst, self.hy)],
            2 * n + (side * 2 + d) * n + c, self.at_y[d])

    def start_x(self, c):
        for d in range(2):
            pl.when(self.has_x[d])(lambda d=d: self.copy_x(d, c).start())

    def start_y(self, k):
        for d in range(2):
            pl.when(self.has_y[d])(lambda d=d: self.copy_y(d, k).start())

    def clear(self):
        rows, cols, z = self.ext.shape
        for d in range(2):
            @pl.when(jnp.logical_not(self.has_x[d]))
            def _(d=d):
                at = 0 if d == 0 else self.hx + self.nx
                self.ext[pl.ds(at, self.hx)] = jnp.zeros((self.hx, cols, z), F32)

            @pl.when(jnp.logical_not(self.has_y[d]))
            def _(d=d):
                at = 0 if d == 0 else self.hy + self.ny
                self.ext[:, pl.ds(at, self.hy)] = jnp.zeros((rows, self.hy, z), F32)

    def forward(self, c):
        for side in range(2):
            @pl.when(self.has_x[1 - side])
            def _(side=side):
                self.copy_x(side, c).wait_recv()
                for d in range(2):
                    pl.when(self.has_y[d])(lambda d=d: self.copy_corner(side, d, c).start())

    def wait_y(self, k):
        for d in range(2):
            pl.when(self.has_y[1 - d])(lambda d=d: self.copy_y(d, k).wait_recv())

    def wait_corner(self, c):
        for side in range(2):
            for d in range(2):
                pl.when(jnp.logical_and(self.has_x[1 - side], self.has_y[1 - d]))(
                    lambda d=d, side=side: self.copy_corner(side, d, c).wait_recv())

    def wait_sends(self):
        for d in range(2):
            for k in range(len(self.bands)):
                pl.when(self.has_y[d])(lambda d=d, k=k: self.copy_y(d, k).wait_send())
            for c in range(len(self.cuts)):
                pl.when(self.has_x[d])(lambda d=d, c=c: self.copy_x(d, c).wait_send())
                for side in range(2):
                    pl.when(jnp.logical_and(self.has_x[1 - side], self.has_y[d]))(
                        lambda d=d, c=c, side=side: self.copy_corner(side, d, c).wait_send())


def split(value):
    high = value.astype(BF16)
    return high, (value - high.astype(F32)).astype(BF16)


def dot(a, b):
    return jnp.dot(a, b, preferred_element_type=F32)


def left(weights, value):
    high, low = split(value)
    return dot(weights, jnp.concatenate([high, low, high], axis=0))


def right(value, high_w, low_w):
    high, low = split(value)
    return dot(high, high_w) + dot(low, high_w) + dot(high, low_w)


STEP = 5
IMG_CUTS = tuple((a, a + STEP) for a in range(0, IMG_X, STEP))
POT_CUTS = ((0, POT_X),)


def brick_bands(bx):
    middle = bx // 2
    return ((0, POT_X), (bx - POT_X, bx), (POT_X, middle), (middle, bx - POT_X))


def tensor_kernel(image, phases_in, table_in, start, wg_in, ws_in, zg_in, zs_in, cond, pot,
                  ext, masked, along, smooth, phases, table, wg, ws, zg, zs, *sems):
    gx, gy = lax.axis_index("gx"), lax.axis_index("gy")
    bx, by, z = phases.shape
    size_x, size_y = bx * lax.axis_size("gx"), by * lax.axis_size("gy")
    wide_y = ext.shape[1]
    rows_x = bx + 2 * SMOOTH
    bands = brick_bands(bx)

    img = Exchange(image, ext, IMG_X, IMG_Y, IMG_CUTS, ((0, bx),), *sems[0:2])
    pots = Exchange(start, pot, POT_X, POT_Y, POT_CUTS, ((0, bx),), *sems[2:4])
    conds = Exchange(None, cond, POT_X, POT_Y, POT_CUTS, bands, *sems[4:6])
    own_image = pltpu.make_async_copy(
        image, ext.at[pl.ds(IMG_X, bx), pl.ds(IMG_Y, by)], sems[6])
    own_start = pltpu.make_async_copy(
        start, pot.at[pl.ds(POT_X, bx), pl.ds(POT_Y, by)], sems[7])

    loads = [
        pltpu.make_async_copy(src, dst, sems[8 + k])
        for k, (src, dst) in enumerate((
            (wg_in, wg), (zg_in, zg), (ws_in, ws), (phases_in, phases), (zs_in, zs),
            (table_in, table)))
    ]
    own_image.start()
    for load in loads:
        load.start()
    greet()
    img.start_x(0)
    img.start_y(0)
    for c in range(1, len(IMG_CUTS)):
        img.start_x(c)
    own_start.start()
    for part in (img, pots, conds):
        part.clear()

    for load in loads[:3]:
        load.wait()
    row_y = gy * by - IMG_Y + lax.broadcasted_iota(jnp.int32, (wide_y, wg.shape[1]), 0)
    inside = jnp.logical_and(row_y >= 0, row_y < size_y)
    for k in range(2):
        part = wg[k * wide_y:(k + 1) * wide_y].astype(F32)
        masked[k * wide_y:(k + 1) * wide_y] = jnp.where(inside, part, 0.0).astype(BF16)
    own_image.wait()

    def derive(row):
        firsts, seconds = [], []
        for j in range(STEP):
            r = row + j
            at = gx * bx + r - SMOOTH
            ok = jnp.logical_and(at >= 0, at < size_x).astype(F32)
            e = [ext[r + t] for t in range(2 * DERIV + 1)]
            a = e[DERIV] * (NEAR[DERIV] * ok)
            b = jnp.zeros_like(a)
            for t in range(1, DERIV + 1):
                a = a + (e[DERIV + t] + e[DERIV - t]) * (NEAR[DERIV + t] * ok)
                b = b + (e[DERIV + t] - e[DERIV - t]) * (SLOPE[DERIV + t] * ok)
            y_a = left(masked[...], a)
            y_b = left(masked[:wide_y], b)
            firsts += [y_b, y_a[wide_y:]]
            seconds.append(y_a[:wide_y])
        first = right(jnp.concatenate(firsts, axis=0), zg[:, :z], zg[:, z:2 * z])
        second = right(jnp.concatenate(seconds, axis=0), zg[:, 2 * z:3 * z], zg[:, 3 * z:])
        for j in range(STEP):
            r = row + j
            g_x = first[2 * j * wide_y:(2 * j + 1) * wide_y]
            g_y = first[(2 * j + 1) * wide_y:(2 * j + 2) * wide_y]
            g_z = second[j * wide_y:(j + 1) * wide_y]
            for f, (p, q) in enumerate(
                ((g_x, g_x), (g_y, g_y), (g_z, g_z), (g_x, g_y), (g_x, g_z), (g_y, g_z))
            ):
                along[f, r] = left(ws[...], p * q)

    def derive_both(low, high):
        def step(k, carry):
            derive(low + k * (high - low))
            return carry
        lax.fori_loop(0, 2, step, 0)

    centre = rows_x // 2
    img.forward(0)
    img.wait_y(0)
    derive_both(centre - STEP, centre)
    tiles_y, tiles_z = by // 8, z // 128

    def smooth_x(known, ready, add):
        def step(n, carry):
            f = n // (tiles_y * tiles_z)
            ys = pl.ds(pl.multiple_of((n // tiles_z) % tiles_y * 8, 8), 8)
            zz = pl.ds(pl.multiple_of(n % tiles_z * 128, 128), 128)
            new = [r in known and r not in ready for r in range(rows_x)]
            v = [along[f, r, ys, zz] if new[r] else None for r in range(rows_x)]
            for i in range(bx):
                c = i + SMOOTH
                terms = [v[c] * WIDE[SMOOTH]] if new[c] else []
                for t in range(1, SMOOTH + 1):
                    pair = [v[r] for r in (c + t, c - t) if new[r]]
                    if pair:
                        terms.append((pair[0] + pair[1] if len(pair) > 1 else pair[0])
                                     * WIDE[SMOOTH + t])
                if terms:
                    total = smooth[f, i, ys, zz] if add else terms.pop(0)
                    for term in terms:
                        total = total + term
                    smooth[f, i, ys, zz] = total
            return carry
        lax.fori_loop(0, 6 * tiles_y * tiles_z, step, 0)

    last = len(IMG_CUTS) - 1
    for c in range(last):
        img.forward(c + 1)
        img.wait_corner(c)
        derive_both(centre - (c + 2) * STEP, centre + (c + 1) * STEP)
    pots.start_x(0)
    pots.start_y(0)
    inner = range(STEP, rows_x - STEP)
    smooth_x(inner, (), False)
    img.wait_corner(last)
    derive_both(0, rows_x - STEP)
    pots.forward(0)
    smooth_x(range(rows_x), inner, True)
    for load in loads[3:]:
        load.wait()

    def finish(rows):
        every = right(
            jnp.concatenate([smooth[f, i] for i in rows for f in range(6)], axis=0),
            zs[:, :z], zs[:, z:])
        for n, i in enumerate(rows):
            s = every[n * 6 * by:(n + 1) * 6 * by]
            jxx, jyy, jzz, jxy, jxz, jyz = (s[f * by:(f + 1) * by] for f in range(6))
            trace = jxx + jyy + jzz
            shift = 0.1 * trace + 1e-06
            a, b, c = jxx + shift, jyy + shift, jzz + shift
            cof = a * b - jxy * jxy
            det = (
                a * (b * c - jyz * jyz)
                - jxy * (jxy * c - jyz * jxz)
                + jxz * (jxy * jyz - b * jxz)
            )
            weight = trace * cof / det
            label = phases[i]
            base = jnp.where(
                label == 0, table[0, 0], jnp.where(label == 1, table[0, 1], table[0, 2]))
            aniso = jnp.where(
                label == 0, table[1, 0], jnp.where(label == 1, table[1, 1], table[1, 2]))
            cond[POT_X + i, POT_Y:POT_Y + by] = base + 0.1 * aniso * weight

    finish([i for low, high in bands[:2] for i in range(low, high)])
    conds.start_x(0)
    conds.start_y(0)
    conds.start_y(1)
    for k in range(2, len(bands)):
        finish(list(range(*bands[k])))
        conds.start_y(k)
    conds.forward(0)

    own_start.wait()
    pots.wait_y(0)
    pots.wait_corner(0)
    for k in range(len(bands)):
        conds.wait_y(k)
    conds.wait_corner(0)
    for part in (img, pots, conds):
        part.wait_sends()


def tensor(image, phases, table, start):
    bx, by, z = phases.shape
    wide_y = by + 2 * IMG_Y
    rows_x = bx + 2 * SMOOTH
    lo, hi = IMG_Y - SMOOTH, wide_y - (IMG_Y - SMOOTH)
    wg = np.concatenate([
        left_weights(band(wide_y, wide_y, 0, NEAR, lo, hi)),
        left_weights(band(wide_y, wide_y, 0, SLOPE, lo, hi)),
    ], axis=0)
    ws = left_weights(band(by, wide_y, IMG_Y, WIDE))
    zg = right_weights(band(z, z, 0, NEAR), band(z, z, 0, SLOPE))
    zs = right_weights(band(z, z, 0, WIDE))
    vmem = pl.BlockSpec(memory_space=pltpu.VMEM)
    anywhere = pl.BlockSpec(memory_space=pl.ANY)
    outer = jax.ShapeDtypeStruct((bx + 2 * POT_X, by + 2 * POT_Y, z), F32)
    sems = []
    for count in (
        Exchange.count(IMG_CUTS, ((0, bx),)),
        Exchange.count(POT_CUTS, ((0, bx),)),
        Exchange.count(POT_CUTS, brick_bands(bx)),
    ):
        sems += [pltpu.SemaphoreType.DMA((count,))] * 2
    return pl.pallas_call(
        tensor_kernel,
        out_shape=[outer, outer],
        in_specs=[anywhere] * 8,
        out_specs=[vmem, vmem],
        scratch_shapes=[
            pltpu.VMEM((bx + 2 * IMG_X, wide_y, z), F32),
            pltpu.VMEM(wg.shape, BF16),
            pltpu.VMEM((6, rows_x, by, z), F32),
            pltpu.VMEM((6, bx, by, z), F32),
            pltpu.VMEM(phases.shape, jnp.int32),
            pltpu.SMEM(table.shape, F32),
        ] + [pltpu.VMEM(w.shape, BF16) for w in (wg, ws, zg, zs)]
        + sems + [pltpu.SemaphoreType.DMA] * 8,
        compiler_params=pltpu.CompilerParams(
            collective_id=0, has_side_effects=True, vmem_limit_bytes=VMEM_LIMIT),
    )(image, phases, table, start, wg, ws, zg, zs)


def harmonic(p, q):
    total = p + q
    return 2.0 * p * q / jnp.where(total > 0, total, 1.0)


def step_of(count):
    return max(n for n in (1, 2, 3, 4) if count % n == 0)


def sweep_kernel(cond_in, start_in, centre, out, cond, start, kx, y0, y1, z0, z1, inv, one, two,
                 *sems):
    rows, wide, z = cond.shape
    get_cond = pltpu.make_async_copy(cond_in, cond, sems[0])
    get_start = pltpu.make_async_copy(start_in, start, sems[1])
    get_cond.start()
    get_start.start()
    get_cond.wait()
    copy = pltpu.make_async_copy(
        cond.at[pl.ds(POT_X, rows - 2 * POT_X), pl.ds(POT_Y, wide - 2 * POT_Y)], centre, sems[2])
    copy.start()
    lane = lax.broadcasted_iota(jnp.int32, (1, wide, z), 2)
    at_low, at_high = lane == 0, lane == z - 1

    def roll_y(v, s):
        return pltpu.roll(v, s % wide, 1)

    def roll_z(v, s):
        return pltpu.roll(v, s % z, 2)

    kx[0] = harmonic(cond[0], cond[1])
    size = 2

    def coefficients(step, carry):
        j = 1 + step * size
        c = cond[pl.ds(j, size)]
        x_up = harmonic(c, cond[pl.ds(j + 1, size)])
        y_up = harmonic(c, roll_y(c, -1))
        z_up = harmonic(c, roll_z(c, -1))
        x_down = jnp.concatenate([kx[j - 1][None], x_up[:size - 1]], axis=0)
        y_down = roll_y(y_up, 1)
        low = jnp.where(at_low, c, roll_z(z_up, 1))
        high = jnp.where(at_high, c, z_up)
        total = x_down + x_up + y_down + y_up + low + high
        kx[pl.ds(j, size)] = x_up
        y0[pl.ds(j, size)] = y_down
        y1[pl.ds(j, size)] = y_up
        z0[pl.ds(j, size)] = low
        z1[pl.ds(j, size)] = high
        inv[pl.ds(j, size)] = 1.0 / jnp.where(total > 0, total, 1.0)
        return carry

    lax.fori_loop(0, (rows - 2) // size, coefficients, 0)
    get_start.wait()

    def sweep(src, dst, shift, cols, first, last):
        size = step_of(last - first)

        def step(k, carry):
            j = first + k * size
            at = pl.ds(j, size)
            p = src[at]
            numer = kx[pl.ds(j - 1, size)] * src[pl.ds(j - 1, size)]
            numer = numer + kx[at] * src[pl.ds(j + 1, size)]
            numer = numer + y0[at] * roll_y(p, 1) + y1[at] * roll_y(p, -1)
            numer = numer + z0[at] * jnp.where(at_low, 1.0, roll_z(p, 1))
            numer = numer + z1[at] * jnp.where(at_high, 0.0, roll_z(p, -1))
            value = numer * inv[at]
            dst[pl.ds(j - shift, size)] = value[:, cols:wide - cols]
            return carry
        lax.fori_loop(0, (last - first) // size, step, 0)

    sweep(start, one, 0, 0, 1, rows - 1)
    sweep(one, two, 0, 0, 2, rows - 2)
    sweep(two, out, POT_X, POT_Y, 3, rows - 3)
    copy.wait()


def sweeps(cond_ext, pot_ext):
    rows, wide, z = cond_ext.shape
    vmem = pl.BlockSpec(memory_space=pltpu.VMEM)
    brick = jax.ShapeDtypeStruct((rows - 2 * POT_X, wide - 2 * POT_Y, z), F32)
    return pl.pallas_call(
        sweep_kernel,
        out_shape=[brick, brick],
        in_specs=[pl.BlockSpec(memory_space=pl.ANY)] * 2,
        out_specs=[pl.BlockSpec(memory_space=pl.ANY), vmem],
        scratch_shapes=[pltpu.VMEM((rows, wide, z), F32)] * 10 + [pltpu.SemaphoreType.DMA] * 3,
        compiler_params=pltpu.CompilerParams(vmem_limit_bytes=VMEM_LIMIT),
    )(cond_ext, pot_ext)


def body(image, phases, phase_table, start_potential):
    cond_ext, pot_ext = tensor(image, phases, phase_table, start_potential)
    conductivity, potential = sweeps(cond_ext, pot_ext)
    return conductivity, potential


def solution(mesh):
    placed = (P("gx", "gy", None), P("gx", "gy", None), P(), P("gx", "gy", None))
    return jax.shard_map(
        body,
        mesh=mesh,
        in_specs=placed,
        out_specs=(P("gx", "gy", None), P("gx", "gy", None)),
        check_vma=False,
    )
```

profile of v0, /device:TPU:3, one launch (start us, length us, event | category | flops | bytes accessed | tf_op | source)
XLA Modules:
  0.0 49.1 jit_solution(2461559531152494718)
XLA Ops:
  0.6 41.7 %shard_map.95 = (f32[22,48,256]{2,1,0:T(8,128)}, f32[22,48,256]{2,1,0:T(8,128)}) custom-call(f32[16,32,256]{2,1,0:T(8,128)} %image.1, s32[16,32,256]{2,1,0:T(8,128)} %phases_in.1, f32[2,3]{1,0:T(2,128)} %table_in.1, f32[16,32,256]{2,1,0:T(8,128)} %start.1, bf16[128,192]{1,0:T(8,128)(2,1)} %constant.8.clone.wg_in, bf16[32,192]{1,0:T(8,128)(2,1)} %constant.9.clone.ws_in, ...), custom_call_target="tpu_custom_call" | custom-call | tf_op jit(solution)/shard_map/pallas_call | solution.py:413
  42.3 6.7 %shard_map.96 = (f32[16,32,256]{2,1,0:T(8,128)}, f32[16,32,256]{2,1,0:T(8,128)}) custom-call(f32[22,48,256]{2,1,0:T(8,128)} %get-tuple-element.4.cond_in, f32[22,48,256]{2,1,0:T(8,128)} %get-tuple-element.5.start_in), custom_call_target="tpu_custom_call" | custom-call | tf_op jit(solution)/shard_map/pallas_call | solution.py:513
where the time goes:
time: 49.2 us; the launch traced here: 49.1 us
  Pallas kernels  48.4 us (98%)
  between operations  0.64 us (1%)
    pallas_call x1, Pallas kernels, tensor(): pl.pallas_call(tensor_kernel, out_shape=[outer, outer], in_specs=[anywher...  41.7 us
    pallas_call x1, Pallas kernels, sweeps(): pl.pallas_call(sweep_kernel, out_shape=[brick, brick], in_specs=[pl.Block...  6.73 us

commit v1 on v0

--- a/solution.py
+++ b/solution.py
@@ -88,16 +88,24 @@
 
 
 class Exchange:
-    def __init__(self, own, ext, hx, hy, cuts, bands, send, recv):
+    def __init__(self, own, ext, hx, hy, cuts, bands, send, recv, middle=False):
         self.ext, self.hx, self.hy, self.cuts, self.bands = ext, hx, hy, cuts, bands
         self.send, self.recv = send, recv
         self.nx, self.ny = ext.shape[0] - 2 * hx, ext.shape[1] - 2 * hy
         self.own = own
         self.has_x, self.has_y, self.at_x, self.at_y = neighbours()
+        gy, half = lax.axis_index("gy"), lax.axis_size("gy") // 2
+        if middle:
+            self.mid = (gy == half, gy == half - 1)
+            self.passes = tuple(
+                jnp.logical_and(has, jnp.logical_not(mid))
+                for has, mid in zip(self.has_y, self.mid))
+        else:
+            self.mid, self.passes = None, self.has_y
 
     @staticmethod
     def count(cuts, bands):
-        return 2 * len(bands) + 6 * len(cuts)
+        return 2 * len(bands) + 8 * len(cuts)
 
     def remote(self, src, dst, index, at):
         return pltpu.make_async_remote_copy(
@@ -143,6 +151,29 @@
             self.ext.at[pl.ds(row, size), pl.ds(dst, self.hy)],
             2 * n + (side * 2 + d) * n + c, self.at_y[d])
 
+    def copy_mid(self, side, d, c):
+        a, b = self.cuts[c]
+        row, size = self.halo_rows(d, (a, b))
+        start = a if d == 0 else self.nx - b
+        at = self.hy + self.ny if side == 1 else 0
+        return self.remote(
+            self.ext.at[pl.ds(self.hx + start, size), pl.ds(at, self.hy)],
+            self.ext.at[pl.ds(row, size), pl.ds(at, self.hy)],
+            6 * len(self.cuts) + 2 * len(self.bands) + d * len(self.cuts) + c, self.at_x[d])
+
+    def each_mid(self, has, action):
+        for side in range(2):
+            for d in range(2):
+                pl.when(jnp.logical_and(self.mid[side], has[d]))(
+                    lambda side=side, d=d: action(side, d))
+
+    def start_mid(self, c):
+        self.each_mid(self.has_x, lambda side, d: self.copy_mid(side, d, c).start())
+
+    def wait_mid(self, c):
+        self.each_mid(
+            self.has_x[::-1], lambda side, d: self.copy_mid(side, d, c).wait_recv())
+
     def start_x(self, c):
         for d in range(2):
             pl.when(self.has_x[d])(lambda d=d: self.copy_x(d, c).start())
@@ -170,7 +201,7 @@
             def _(side=side):
                 self.copy_x(side, c).wait_recv()
                 for d in range(2):
-                    pl.when(self.has_y[d])(lambda d=d: self.copy_corner(side, d, c).start())
+                    pl.when(self.passes[d])(lambda d=d: self.copy_corner(side, d, c).start())
 
     def wait_y(self, k):
         for d in range(2):
@@ -179,8 +210,10 @@
     def wait_corner(self, c):
         for side in range(2):
             for d in range(2):
-                pl.when(jnp.logical_and(self.has_x[1 - side], self.has_y[1 - d]))(
+                pl.when(jnp.logical_and(self.has_x[1 - side], self.passes[1 - d]))(
                     lambda d=d, side=side: self.copy_corner(side, d, c).wait_recv())
+        if self.mid is not None:
+            self.wait_mid(c)
 
     def wait_sends(self):
         for d in range(2):
@@ -189,8 +222,12 @@
             for c in range(len(self.cuts)):
                 pl.when(self.has_x[d])(lambda d=d, c=c: self.copy_x(d, c).wait_send())
                 for side in range(2):
-                    pl.when(jnp.logical_and(self.has_x[1 - side], self.has_y[d]))(
+                    pl.when(jnp.logical_and(self.has_x[1 - side], self.passes[d]))(
                         lambda d=d, c=c, side=side: self.copy_corner(side, d, c).wait_send())
+        if self.mid is not None:
+            for c in range(len(self.cuts)):
+                self.each_mid(
+                    self.has_x, lambda side, d, c=c: self.copy_mid(side, d, c).wait_send())
 
 
 def split(value):
@@ -231,7 +268,7 @@
     rows_x = bx + 2 * SMOOTH
     bands = brick_bands(bx)
 
-    img = Exchange(image, ext, IMG_X, IMG_Y, IMG_CUTS, ((0, bx),), *sems[0:2])
+    img = Exchange(image, ext, IMG_X, IMG_Y, IMG_CUTS, ((0, bx),), *sems[0:2], middle=True)
     pots = Exchange(start, pot, POT_X, POT_Y, POT_CUTS, ((0, bx),), *sems[2:4])
     conds = Exchange(None, cond, POT_X, POT_Y, POT_CUTS, bands, *sems[4:6])
     own_image = pltpu.make_async_copy(
@@ -301,8 +338,10 @@
         lax.fori_loop(0, 2, step, 0)
 
     centre = rows_x // 2
+    img.wait_y(0)
+    for c in range(len(IMG_CUTS)):
+        img.start_mid(c)
     img.forward(0)
-    img.wait_y(0)
     derive_both(centre - STEP, centre)
     tiles_y, tiles_z = by // 8, z // 128
 

time: 49.2 us -> 49.8 us (1.012)
  no operation moved by 1% of the time
where the time goes in v1:
time: 49.8 us; the launch traced here: 49.4 us
  Pallas kernels  48.7 us (98%)
  between operations  0.64 us (1%)
    pallas_call x1, Pallas kernels, tensor(): pl.pallas_call(tensor_kernel, out_shape=[outer, outer], in_specs=[anywher...  42 us
    pallas_call x1, Pallas kernels, sweeps(): pl.pallas_call(sweep_kernel, out_shape=[brick, brick], in_specs=[pl.Block...  6.73 us

profile of v1, /device:TPU:3, one launch (start us, length us, event | category | flops | bytes accessed | tf_op | source)
XLA Modules:
  0.0 49.4 jit_solution(16408807025386438584)
XLA Ops:
  0.6 42.0 %shard_map.95 = (f32[22,48,256]{2,1,0:T(8,128)}, f32[22,48,256]{2,1,0:T(8,128)}) custom-call(f32[16,32,256]{2,1,0:T(8,128)} %image.1, s32[16,32,256]{2,1,0:T(8,128)} %phases_in.1, f32[2,3]{1,0:T(2,128)} %table_in.1, f32[16,32,256]{2,1,0:T(8,128)} %start.1, bf16[128,192]{1,0:T(8,128)(2,1)} %constant.8.clone.wg_in, bf16[32,192]{1,0:T(8,128)(2,1)} %constant.9.clone.ws_in, ...), custom_call_target="tpu_custom_call" | custom-call | tf_op jit(solution)/shard_map/pallas_call | solution.py:452
  42.6 6.7 %shard_map.96 = (f32[16,32,256]{2,1,0:T(8,128)}, f32[16,32,256]{2,1,0:T(8,128)}) custom-call(f32[22,48,256]{2,1,0:T(8,128)} %get-tuple-element.4.cond_in, f32[22,48,256]{2,1,0:T(8,128)} %get-tuple-element.5.start_in), custom_call_target="tpu_custom_call" | custom-call | tf_op jit(solution)/shard_map/pallas_call | solution.py:552

commit v2 on v1

--- a/solution.py
+++ b/solution.py
@@ -19,7 +19,7 @@
 POT_X = SWEEPS
 POT_Y = 8
 MESH = pl.DeviceIdType.MESH
-VMEM_LIMIT = 58 * 1024 * 1024
+VMEM_LIMIT = 32 * 1024 * 1024
 F32 = jnp.float32
 BF16 = jnp.bfloat16
 
@@ -58,6 +58,14 @@
 def left_weights(matrix):
     high, low = halves(matrix)
     return np.concatenate([high, high, low], axis=1)
+
+
+def pair_weights(matrix):
+    high, low = halves(matrix)
+    none = np.zeros_like(high)
+    return np.block([
+        [high, high, none, none], [low, none, none, none],
+        [none, none, high, high], [none, none, low, none]])
 
 
 def right_weights(*matrices):
@@ -117,16 +125,15 @@
             return self.ext.at[pl.ds(self.hx + row, rows), pl.ds(self.hy + col, cols)]
         return self.own.at[pl.ds(row, rows), pl.ds(col, cols)]
 
-    def halo_rows(self, d, cut):
-        a, b = cut
+    def halo_rows(self, d, c):
+        size = self.cuts[0][1]
         if d == 0:
-            return self.nx + self.hx + a, b - a
-        return self.hx - b, b - a
+            return self.nx + self.hx + c * size, size
+        return self.hx - (c + 1) * size, size
 
     def copy_x(self, d, c):
-        a, b = self.cuts[c]
-        row, size = self.halo_rows(d, (a, b))
-        start = a if d == 0 else self.nx - b
+        row, size = self.halo_rows(d, c)
+        start = c * size if d == 0 else self.nx - (c + 1) * size
         return self.remote(
             self.brick(start, size, 0, self.ny),
             self.ext.at[pl.ds(row, size), pl.ds(self.hy, self.ny)],
@@ -142,7 +149,7 @@
             6 * len(self.cuts) + d * len(self.bands) + k, self.at_y[d])
 
     def copy_corner(self, side, d, c):
-        row, size = self.halo_rows(side, self.cuts[c])
+        row, size = self.halo_rows(side, c)
         src = self.hy if d == 0 else self.ny
         dst = self.hy + self.ny if d == 0 else 0
         n = len(self.cuts)
@@ -152,9 +159,8 @@
             2 * n + (side * 2 + d) * n + c, self.at_y[d])
 
     def copy_mid(self, side, d, c):
-        a, b = self.cuts[c]
-        row, size = self.halo_rows(d, (a, b))
-        start = a if d == 0 else self.nx - b
+        row, size = self.halo_rows(d, c)
+        start = c * size if d == 0 else self.nx - (c + 1) * size
         at = self.hy + self.ny if side == 1 else 0
         return self.remote(
             self.ext.at[pl.ds(self.hx + start, size), pl.ds(at, self.hy)],
@@ -255,12 +261,11 @@
 
 
 def brick_bands(bx):
-    middle = bx // 2
-    return ((0, POT_X), (bx - POT_X, bx), (POT_X, middle), (middle, bx - POT_X))
+    return ((0, POT_X), (bx - POT_X, bx), (POT_X, bx - POT_X))
 
 
 def tensor_kernel(image, phases_in, table_in, start, wg_in, ws_in, zg_in, zs_in, cond, pot,
-                  ext, masked, along, smooth, phases, table, wg, ws, zg, zs, *sems):
+                  ext, za, zb, grads, masked, along, smooth, phases, table, wg, ws, zg, zs, *sems):
     gx, gy = lax.axis_index("gx"), lax.axis_index("gy")
     bx, by, z = phases.shape
     size_x, size_y = bx * lax.axis_size("gx"), by * lax.axis_size("gy")
@@ -303,46 +308,60 @@
         masked[k * wide_y:(k + 1) * wide_y] = jnp.where(inside, part, 0.0).astype(BF16)
     own_image.wait()
 
-    def derive(row):
-        firsts, seconds = [], []
-        for j in range(STEP):
-            r = row + j
+    def along_z(row, rows, col, cols):
+        size = rows * cols
+        high, low = split(ext[pl.ds(row, rows), pl.ds(col, cols)].reshape(size, z))
+        for k, to in enumerate((za, zb)):
+            hw, lw = zg[:, 2 * k * z:(2 * k + 1) * z], zg[:, (2 * k + 1) * z:(2 * k + 2) * z]
+            out = dot(high, hw) + dot(low, hw) + dot(high, lw)
+            to[pl.ds(row, rows), pl.ds(col, cols)] = out.reshape(rows, cols, z)
+
+    def loop(count, action):
+        lax.fori_loop(0, count, lambda k, carry: (action(k), carry)[1], 0)
+
+    def gradients(rows, slot):
+        for n, r in enumerate(rows):
             at = gx * bx + r - SMOOTH
             ok = jnp.logical_and(at >= 0, at < size_x).astype(F32)
-            e = [ext[r + t] for t in range(2 * DERIV + 1)]
-            a = e[DERIV] * (NEAR[DERIV] * ok)
-            b = jnp.zeros_like(a)
+            a = [za[r + t] for t in range(2 * DERIV + 1)]
+            b = [zb[r + t] for t in range(2 * DERIV + 1)]
+            a_n, b_n = a[DERIV] * (NEAR[DERIV] * ok), b[DERIV] * (NEAR[DERIV] * ok)
+            a_s = None
             for t in range(1, DERIV + 1):
-                a = a + (e[DERIV + t] + e[DERIV - t]) * (NEAR[DERIV + t] * ok)
-                b = b + (e[DERIV + t] - e[DERIV - t]) * (SLOPE[DERIV + t] * ok)
-            y_a = left(masked[...], a)
-            y_b = left(masked[:wide_y], b)
-            firsts += [y_b, y_a[wide_y:]]
-            seconds.append(y_a[:wide_y])
-        first = right(jnp.concatenate(firsts, axis=0), zg[:, :z], zg[:, z:2 * z])
-        second = right(jnp.concatenate(seconds, axis=0), zg[:, 2 * z:3 * z], zg[:, 3 * z:])
-        for j in range(STEP):
-            r = row + j
-            g_x = first[2 * j * wide_y:(2 * j + 1) * wide_y]
-            g_y = first[(2 * j + 1) * wide_y:(2 * j + 2) * wide_y]
-            g_z = second[j * wide_y:(j + 1) * wide_y]
-            for f, (p, q) in enumerate(
-                ((g_x, g_x), (g_y, g_y), (g_z, g_z), (g_x, g_y), (g_x, g_z), (g_y, g_z))
-            ):
-                along[f, r] = left(ws[...], p * q)
-
-    def derive_both(low, high):
-        def step(k, carry):
-            derive(low + k * (high - low))
-            return carry
-        lax.fori_loop(0, 2, step, 0)
-
-    centre = rows_x // 2
-    img.wait_y(0)
-    for c in range(len(IMG_CUTS)):
-        img.start_mid(c)
-    img.forward(0)
-    derive_both(centre - STEP, centre)
+                near, slope = NEAR[DERIV + t] * ok, SLOPE[DERIV + t] * ok
+                a_n = a_n + (a[DERIV + t] + a[DERIV - t]) * near
+                b_n = b_n + (b[DERIV + t] + b[DERIV - t]) * near
+                term = (a[DERIV + t] - a[DERIV - t]) * slope
+                a_s = term if a_s is None else a_s + term
+            grads[slot + 3 * n] = left(masked[:wide_y], a_s)
+            grads[slot + 3 * n + 1] = left(masked[wide_y:], a_n)
+            grads[slot + 3 * n + 2] = left(masked[:wide_y], b_n)
+
+    def products(rows, slot):
+        for n, r in enumerate(rows):
+            g = [grads[slot + 3 * n + k] for k in range(3)]
+            pairs = ((0, 0), (1, 1), (2, 2), (0, 1), (0, 2), (1, 2))
+            for f in range(0, 6, 2):
+                parts = []
+                for p, q in pairs[f:f + 2]:
+                    parts += split(g[p] * g[q])
+                out = dot(ws[...], jnp.concatenate(parts, axis=0))
+                along[f, r] = out[:by] + out[by:2 * by]
+                along[f + 1, r] = out[2 * by:3 * by] + out[3 * by:]
+
+    centre, chunks = rows_x // 2, len(IMG_CUTS)
+
+    def pair_of(k):
+        part, j = k // STEP, k % STEP
+        return centre - (part + 1) * STEP + j, centre + part * STEP + j
+
+    def derive(part):
+        for j in range(STEP + 1):
+            if j < STEP:
+                gradients(pair_of(part * STEP + j), 6 * j)
+            if j > 0:
+                products(pair_of(part * STEP + j - 1), 6 * (j - 1))
+
     tiles_y, tiles_z = by // 8, z // 128
 
     def smooth_x(known, ready, add):
@@ -368,29 +387,47 @@
             return carry
         lax.fori_loop(0, 6 * tiles_y * tiles_z, step, 0)
 
-    last = len(IMG_CUTS) - 1
-    for c in range(last):
-        img.forward(c + 1)
-        img.wait_corner(c)
-        derive_both(centre - (c + 2) * STEP, centre + (c + 1) * STEP)
-    pots.start_x(0)
-    pots.start_y(0)
-    inner = range(STEP, rows_x - STEP)
-    smooth_x(inner, (), False)
-    img.wait_corner(last)
-    derive_both(0, rows_x - STEP)
+    along_z(IMG_X, bx, IMG_Y, by)
+    img.wait_y(0)
+    for c in range(chunks):
+        img.start_mid(c)
+    along_z(IMG_X, bx, 0, IMG_Y)
+    along_z(IMG_X, bx, IMG_Y + by, IMG_Y)
+    img.forward(0)
+    inner = [r for r in range(STEP, rows_x - STEP)]
+
+    def segment(part):
+        @pl.when(part == chunks)
+        def _():
+            pots.start_x(0)
+            pots.start_y(0)
+            smooth_x(inner, (), False)
+
+        @pl.when(part > 0)
+        def _():
+            c = part - 1
+            pl.when(part < chunks)(lambda: img.forward(c + 1))
+            img.wait_corner(c)
+            along_z(bx + IMG_X + c * STEP, STEP, 0, wide_y)
+            along_z(IMG_X - (c + 1) * STEP, STEP, 0, wide_y)
+        derive(part)
+
+    loop(chunks + 1, segment)
     pots.forward(0)
     smooth_x(range(rows_x), inner, True)
     for load in loads[3:]:
         load.wait()
 
-    def finish(rows):
+    def along_z_last(rows):
         every = right(
             jnp.concatenate([smooth[f, i] for i in rows for f in range(6)], axis=0),
             zs[:, :z], zs[:, z:])
+        grads[:6, :by] = every[:6 * by].reshape(6, by, z)
+        grads[:6, by:2 * by] = every[6 * by:].reshape(6, by, z)
+
+    def weigh(rows):
         for n, i in enumerate(rows):
-            s = every[n * 6 * by:(n + 1) * 6 * by]
-            jxx, jyy, jzz, jxy, jxz, jyz = (s[f * by:(f + 1) * by] for f in range(6))
+            jxx, jyy, jzz, jxy, jxz, jyz = (grads[f, n * by:(n + 1) * by] for f in range(6))
             trace = jxx + jyy + jzz
             shift = 0.1 * trace + 1e-06
             a, b, c = jxx + shift, jyy + shift, jzz + shift
@@ -408,13 +445,21 @@
                 label == 0, table[1, 0], jnp.where(label == 1, table[1, 1], table[1, 2]))
             cond[POT_X + i, POT_Y:POT_Y + by] = base + 0.1 * aniso * weight
 
-    finish([i for low, high in bands[:2] for i in range(low, high)])
-    conds.start_x(0)
-    conds.start_y(0)
-    conds.start_y(1)
-    for k in range(2, len(bands)):
-        finish(list(range(*bands[k])))
-        conds.start_y(k)
+    def rows_of(k):
+        return k, bx - 1 - k
+
+    def finish(k):
+        weigh(rows_of(jnp.maximum(k - 1, 0)))
+        along_z_last(rows_of(jnp.minimum(k, bx // 2 - 1)))
+
+        @pl.when(k == POT_X)
+        def _():
+            conds.start_x(0)
+            conds.start_y(0)
+            conds.start_y(1)
+
+    loop(bx // 2 + 1, finish)
+    conds.start_y(2)
     conds.forward(0)
 
     own_start.wait()
@@ -436,11 +481,11 @@
         left_weights(band(wide_y, wide_y, 0, NEAR, lo, hi)),
         left_weights(band(wide_y, wide_y, 0, SLOPE, lo, hi)),
     ], axis=0)
-    ws = left_weights(band(by, wide_y, IMG_Y, WIDE))
+    ws = pair_weights(band(by, wide_y, IMG_Y, WIDE))
     zg = right_weights(band(z, z, 0, NEAR), band(z, z, 0, SLOPE))
     zs = right_weights(band(z, z, 0, WIDE))
     vmem = pl.BlockSpec(memory_space=pltpu.VMEM)
-    anywhere = pl.BlockSpec(memory_space=pl.ANY)
+    anywhere = pl.BlockSpec(memory_space=pltpu.HBM)
     outer = jax.ShapeDtypeStruct((bx + 2 * POT_X, by + 2 * POT_Y, z), F32)
     sems = []
     for count in (
@@ -456,6 +501,9 @@
         out_specs=[vmem, vmem],
         scratch_shapes=[
             pltpu.VMEM((bx + 2 * IMG_X, wide_y, z), F32),
+            pltpu.VMEM((bx + 2 * IMG_X, wide_y, z), F32),
+            pltpu.VMEM((bx + 2 * IMG_X, wide_y, z), F32),
+            pltpu.VMEM((6 * STEP, wide_y, z), F32),
             pltpu.VMEM(wg.shape, BF16),
             pltpu.VMEM((6, rows_x, by, z), F32),
             pltpu.VMEM((6, bx, by, z), F32),
@@ -465,7 +513,8 @@
         + sems + [pltpu.SemaphoreType.DMA] * 8,
         compiler_params=pltpu.CompilerParams(
             collective_id=0, has_side_effects=True, vmem_limit_bytes=VMEM_LIMIT),
-    )(image, phases, table, start, wg, ws, zg, zs)
+    )(*(pltpu.with_memory_space_constraint(jnp.asarray(x), pltpu.HBM)
+        for x in (image, phases, table, start, wg, ws, zg, zs)))
 
 
 def harmonic(p, q):
@@ -477,16 +526,11 @@
     return max(n for n in (1, 2, 3, 4) if count % n == 0)
 
 
-def sweep_kernel(cond_in, start_in, centre, out, cond, start, kx, y0, y1, z0, z1, inv, one, two,
+def sweep_kernel(cond, start, centre, out, kx, y0, y1, z0, z1, inv, one, two,
                  *sems):
     rows, wide, z = cond.shape
-    get_cond = pltpu.make_async_copy(cond_in, cond, sems[0])
-    get_start = pltpu.make_async_copy(start_in, start, sems[1])
-    get_cond.start()
-    get_start.start()
-    get_cond.wait()
     copy = pltpu.make_async_copy(
-        cond.at[pl.ds(POT_X, rows - 2 * POT_X), pl.ds(POT_Y, wide - 2 * POT_Y)], centre, sems[2])
+        cond.at[pl.ds(POT_X, rows - 2 * POT_X), pl.ds(POT_Y, wide - 2 * POT_Y)], centre, sems[0])
     copy.start()
     lane = lax.broadcasted_iota(jnp.int32, (1, wide, z), 2)
     at_low, at_high = lane == 0, lane == z - 1
@@ -520,7 +564,6 @@
         return carry
 
     lax.fori_loop(0, (rows - 2) // size, coefficients, 0)
-    get_start.wait()
 
     def sweep(src, dst, shift, cols, first, last):
         size = step_of(last - first)
@@ -552,9 +595,9 @@
     return pl.pallas_call(
         sweep_kernel,
         out_shape=[brick, brick],
-        in_specs=[pl.BlockSpec(memory_space=pl.ANY)] * 2,
+        in_specs=[vmem] * 2,
         out_specs=[pl.BlockSpec(memory_space=pl.ANY), vmem],
-        scratch_shapes=[pltpu.VMEM((rows, wide, z), F32)] * 10 + [pltpu.SemaphoreType.DMA] * 3,
+        scratch_shapes=[pltpu.VMEM((rows, wide, z), F32)] * 8 + [pltpu.SemaphoreType.DMA],
         compiler_params=pltpu.CompilerParams(vmem_limit_bytes=VMEM_LIMIT),
     )(cond_ext, pot_ext)
 

time: 49.8 us -> 45.6 us (0.916)
  Pallas kernels: 48.7 us -> 44.6 us
    pallas_call x1, Pallas kernels: 42 us -> 39.1 us  [tensor(): pl.pallas_call(tensor_kernel, out_shape=[outer, outer], in_specs=[anywher...]
    pallas_call x1, Pallas kernels: 6.73 us -> 5.46 us  [sweeps(): pl.pallas_call(sweep_kernel, out_shape=[brick, brick], in_specs=[vmem] *...]
where the time goes in v2:
time: 45.6 us; the launch traced here: 45.2 us
  Pallas kernels  44.6 us (98%)
  between operations  0.64 us (1%)
    pallas_call x1, Pallas kernels, tensor(): pl.pallas_call(tensor_kernel, out_shape=[outer, outer], in_specs=[anywher...  39.1 us
    pallas_call x1, Pallas kernels, sweeps(): pl.pallas_call(sweep_kernel, out_shape=[brick, brick], in_specs=[vmem] *...  5.46 us

profile of v2, /device:TPU:3, one launch (start us, length us, event | category | flops | bytes accessed | tf_op | source)
XLA Modules:
  0.0 45.2 jit_solution(3689341251169714112)
XLA Ops:
  0.6 39.1 %shard_map.95 = (f32[22,48,256]{2,1,0:T(8,128)S(1)}, f32[22,48,256]{2,1,0:T(8,128)S(1)}) custom-call(f32[16,32,256]{2,1,0:T(8,128)} %image.1, s32[16,32,256]{2,1,0:T(8,128)} %phases_in.1, f32[2,3]{1,0:T(2,128)} %table_in.1, f32[16,32,256]{2,1,0:T(8,128)} %start.1, bf16[128,192]{1,0:T(8,128)(2,1)} %constant.8.clone.wg_in, ...), custom_call_target="tpu_custom_call" | custom-call | tf_op jit(solution)/shard_map/pallas_call | solution.py:497
  39.7 5.5 %shard_map.96 = (f32[16,32,256]{2,1,0:T(8,128)}, f32[16,32,256]{2,1,0:T(8,128)}) custom-call(f32[22,48,256]{2,1,0:T(8,128)S(1)} %get-tuple-element.4.cond, f32[22,48,256]{2,1,0:T(8,128)S(1)} %get-tuple-element.5.start), custom_call_target="tpu_custom_call" | custom-call | tf_op jit(solution)/shard_map/pallas_call | solution.py:595

commit v3 on v2

--- a/solution.py
+++ b/solution.py
@@ -88,11 +88,15 @@
 def greet():
     has_x, has_y, at_x, at_y = neighbours()
     barrier = pltpu.get_barrier_semaphore()
-    for has, at in zip(has_x + has_y, at_x + at_y):
+    known = list(zip(has_x + has_y, at_x + at_y))
+    for d in range(2):
+        for e in range(2):
+            known.append((jnp.logical_and(has_x[d], has_y[e]), (at_x[d][0], at_y[e][1])))
+    for has, at in known:
         @pl.when(has)
         def _(at=at):
             pl.semaphore_signal(barrier, inc=1, device_id=at, device_id_type=MESH)
-    pl.semaphore_wait(barrier, sum(has.astype(jnp.int32) for has in has_x + has_y))
+    pl.semaphore_wait(barrier, sum(has.astype(jnp.int32) for has, _ in known))
 
 
 class Exchange:
@@ -158,6 +162,32 @@
             self.ext.at[pl.ds(row, size), pl.ds(dst, self.hy)],
             2 * n + (side * 2 + d) * n + c, self.at_y[d])
 
+    def copy_diagonal(self, d, e):
+        row, size = self.halo_rows(d, 0)
+        return self.remote(
+            self.brick(0 if d == 0 else self.nx - size, size,
+                       0 if e == 0 else self.ny - self.hy, self.hy),
+            self.ext.at[pl.ds(row, size),
+                        pl.ds(self.hy + self.ny if e == 0 else 0, self.hy)],
+            2 * len(self.cuts) + 2 * d + e, (self.at_x[d][0], self.at_y[e][1]))
+
+    def each_diagonal(self, has_x, has_y, action):
+        for d in range(2):
+            for e in range(2):
+                pl.when(jnp.logical_and(has_x[d], has_y[e]))(
+                    lambda d=d, e=e: action(self.copy_diagonal(d, e)))
+
+    def start_diagonal(self):
+        self.each_diagonal(self.has_x, self.has_y, lambda copy: copy.start())
+
+    def wait_all(self):
+        for d in range(2):
+            pl.when(self.has_x[1 - d])(lambda d=d: self.copy_x(d, 0).wait_recv())
+        for k in range(len(self.bands)):
+            self.wait_y(k)
+        self.each_diagonal(
+            self.has_x[::-1], self.has_y[::-1], lambda copy: copy.wait_recv())
+
     def copy_mid(self, side, d, c):
         row, size = self.halo_rows(d, c)
         start = c * size if d == 0 else self.nx - (c + 1) * size
@@ -184,6 +214,10 @@
         for d in range(2):
             pl.when(self.has_x[d])(lambda d=d: self.copy_x(d, c).start())
 
+    def sent_x(self, c):
+        for d in range(2):
+            pl.when(self.has_x[d])(lambda d=d: self.copy_x(d, c).wait_send())
+
     def start_y(self, k):
         for d in range(2):
             pl.when(self.has_y[d])(lambda d=d: self.copy_y(d, k).start())
@@ -225,15 +259,17 @@
         for d in range(2):
             for k in range(len(self.bands)):
                 pl.when(self.has_y[d])(lambda d=d, k=k: self.copy_y(d, k).wait_send())
-            for c in range(len(self.cuts)):
-                pl.when(self.has_x[d])(lambda d=d, c=c: self.copy_x(d, c).wait_send())
-                for side in range(2):
+        self.sent_x(len(self.cuts) - 1)
+        if self.mid is None:
+            self.each_diagonal(self.has_x, self.has_y, lambda copy: copy.wait_send())
+            return
+        for c in range(len(self.cuts)):
+            for side in range(2):
+                for d in range(2):
                     pl.when(jnp.logical_and(self.has_x[1 - side], self.passes[d]))(
                         lambda d=d, c=c, side=side: self.copy_corner(side, d, c).wait_send())
-        if self.mid is not None:
-            for c in range(len(self.cuts)):
-                self.each_mid(
-                    self.has_x, lambda side, d, c=c: self.copy_mid(side, d, c).wait_send())
+            self.each_mid(
+                self.has_x, lambda side, d, c=c: self.copy_mid(side, d, c).wait_send())
 
 
 def split(value):
@@ -256,12 +292,17 @@
 
 
 STEP = 5
+BEFORE = 0.5
 IMG_CUTS = tuple((a, a + STEP) for a in range(0, IMG_X, STEP))
 POT_CUTS = ((0, POT_X),)
 
 
 def brick_bands(bx):
-    return ((0, POT_X), (bx - POT_X, bx), (POT_X, bx - POT_X))
+    low = [0, POT_X, 2 * POT_X]
+    bands = []
+    for a, b in zip(low, low[1:]):
+        bands += [(a, b), (bx - b, bx - a)]
+    return tuple(bands) + ((low[-1], bx - low[-1]),)
 
 
 def tensor_kernel(image, phases_in, table_in, start, wg_in, ws_in, zg_in, zs_in, cond, pot,
@@ -293,8 +334,6 @@
     greet()
     img.start_x(0)
     img.start_y(0)
-    for c in range(1, len(IMG_CUTS)):
-        img.start_x(c)
     own_start.start()
     for part in (img, pots, conds):
         part.clear()
@@ -364,12 +403,13 @@
 
     tiles_y, tiles_z = by // 8, z // 128
 
-    def smooth_x(known, ready, add):
-        def step(n, carry):
+    def smooth_x(known, ready, tiles, first=0, last=1):
+        new = [r in known and r not in ready for r in range(rows_x)]
+
+        def tile(n):
             f = n // (tiles_y * tiles_z)
             ys = pl.ds(pl.multiple_of((n // tiles_z) % tiles_y * 8, 8), 8)
             zz = pl.ds(pl.multiple_of(n % tiles_z * 128, 128), 128)
-            new = [r in known and r not in ready for r in range(rows_x)]
             v = [along[f, r, ys, zz] if new[r] else None for r in range(rows_x)]
             for i in range(bx):
                 c = i + SMOOTH
@@ -380,54 +420,71 @@
                         terms.append((pair[0] + pair[1] if len(pair) > 1 else pair[0])
                                      * WIDE[SMOOTH + t])
                 if terms:
-                    total = smooth[f, i, ys, zz] if add else terms.pop(0)
+                    total = smooth[f, i, ys, zz] if ready else terms.pop(0)
                     for term in terms:
                         total = total + term
                     smooth[f, i, ys, zz] = total
-            return carry
-        lax.fori_loop(0, 6 * tiles_y * tiles_z, step, 0)
+
+        def step(n):
+            for k in range(tiles):
+                tile(n * tiles + k)
+        count = 6 * tiles_y * tiles_z // tiles
+        begin, end = (round(count * part) for part in (first, last))
+        lax.fori_loop(begin, end, lambda n, carry: (step(n), carry)[1], 0)
 
     along_z(IMG_X, bx, IMG_Y, by)
+    img.sent_x(0)
+    img.start_x(1)
     img.wait_y(0)
-    for c in range(chunks):
-        img.start_mid(c)
+    img.start_mid(0)
+    img.forward(0)
     along_z(IMG_X, bx, 0, IMG_Y)
     along_z(IMG_X, bx, IMG_Y + by, IMG_Y)
-    img.forward(0)
-    inner = [r for r in range(STEP, rows_x - STEP)]
+    img.sent_x(1)
+    img.start_x(2)
+    img.start_mid(1)
+    img.start_mid(2)
+    core = range((chunks - 1) * STEP, rows_x - (chunks - 1) * STEP)
+    inner = range(STEP, rows_x - STEP)
 
     def segment(part):
         @pl.when(part == chunks)
         def _():
-            pots.start_x(0)
             pots.start_y(0)
-            smooth_x(inner, (), False)
+            pots.start_diagonal()
+            smooth_x(inner, core, 4)
 
         @pl.when(part > 0)
         def _():
             c = part - 1
+            pl.when(part == chunks - 1)(lambda: smooth_x(core, (), 2, 0, BEFORE))
             pl.when(part < chunks)(lambda: img.forward(c + 1))
+
+            @pl.when(part == chunks - 1)
+            def _():
+                pots.start_x(0)
+                smooth_x(core, (), 2, BEFORE, 1)
             img.wait_corner(c)
             along_z(bx + IMG_X + c * STEP, STEP, 0, wide_y)
             along_z(IMG_X - (c + 1) * STEP, STEP, 0, wide_y)
         derive(part)
 
     loop(chunks + 1, segment)
-    pots.forward(0)
-    smooth_x(range(rows_x), inner, True)
+    smooth_x(range(rows_x), inner, 4)
     for load in loads[3:]:
         load.wait()
 
-    def along_z_last(rows):
+    def along_z_last(rows, slot):
         every = right(
             jnp.concatenate([smooth[f, i] for i in rows for f in range(6)], axis=0),
             zs[:, :z], zs[:, z:])
-        grads[:6, :by] = every[:6 * by].reshape(6, by, z)
-        grads[:6, by:2 * by] = every[6 * by:].reshape(6, by, z)
-
-    def weigh(rows):
+        grads[slot:slot + 6, :by] = every[:6 * by].reshape(6, by, z)
+        grads[slot:slot + 6, by:2 * by] = every[6 * by:].reshape(6, by, z)
+
+    def weigh(rows, slot):
         for n, i in enumerate(rows):
-            jxx, jyy, jzz, jxy, jxz, jyz = (grads[f, n * by:(n + 1) * by] for f in range(6))
+            jxx, jyy, jzz, jxy, jxz, jyz = (
+                grads[slot + f, n * by:(n + 1) * by] for f in range(6))
             trace = jxx + jyy + jzz
             shift = 0.1 * trace + 1e-06
             a, b, c = jxx + shift, jyy + shift, jzz + shift
@@ -448,26 +505,25 @@
     def rows_of(k):
         return k, bx - 1 - k
 
-    def finish(k):
-        weigh(rows_of(jnp.maximum(k - 1, 0)))
-        along_z_last(rows_of(jnp.minimum(k, bx // 2 - 1)))
-
-        @pl.when(k == POT_X)
-        def _():
+    pairs = bx // 2
+    for k in range(pairs + 1):
+        if k < pairs:
+            along_z_last(rows_of(k), 6 * (k % STEP))
+        if k > 0:
+            weigh(rows_of(k - 1), 6 * ((k - 1) % STEP))
+        if k == POT_X:
             conds.start_x(0)
+            conds.start_diagonal()
             conds.start_y(0)
             conds.start_y(1)
-
-    loop(bx // 2 + 1, finish)
-    conds.start_y(2)
-    conds.forward(0)
+        if k == 2 * POT_X:
+            conds.start_y(2)
+            conds.start_y(3)
+    conds.start_y(4)
 
     own_start.wait()
-    pots.wait_y(0)
-    pots.wait_corner(0)
-    for k in range(len(bands)):
-        conds.wait_y(k)
-    conds.wait_corner(0)
+    pots.wait_all()
+    conds.wait_all()
     for part in (img, pots, conds):
         part.wait_sends()
 

time: 45.6 us -> 42.7 us (0.936)
  Pallas kernels: 44.6 us -> 41.8 us
    pallas_call x1, Pallas kernels: 39.1 us -> 36.3 us  [tensor(): pl.pallas_call(tensor_kernel, out_shape=[outer, outer], in_specs=[anywher...]
where the time goes in v3:
time: 42.7 us; the launch traced here: 42.4 us
  Pallas kernels  41.8 us (98%)
  between operations  0.64 us (1%)
    pallas_call x1, Pallas kernels, tensor(): pl.pallas_call(tensor_kernel, out_shape=[outer, outer], in_specs=[anywher...  36.3 us
    pallas_call x1, Pallas kernels, sweeps(): pl.pallas_call(sweep_kernel, out_shape=[brick, brick], in_specs=[vmem] *...  5.46 us

profile of v3, /device:TPU:3, one launch (start us, length us, event | category | flops | bytes accessed | tf_op | source)
XLA Modules:
  0.0 42.4 jit_solution(10497470594803652590)
XLA Ops:
  0.6 36.3 %shard_map.95 = (f32[22,48,256]{2,1,0:T(8,128)S(1)}, f32[22,48,256]{2,1,0:T(8,128)S(1)}) custom-call(f32[16,32,256]{2,1,0:T(8,128)} %image.1, s32[16,32,256]{2,1,0:T(8,128)} %phases_in.1, f32[2,3]{1,0:T(2,128)} %table_in.1, f32[16,32,256]{2,1,0:T(8,128)} %start.1, bf16[128,192]{1,0:T(8,128)(2,1)} %constant.8.clone.wg_in, ...), custom_call_target="tpu_custom_call" | custom-call | tf_op jit(solution)/shard_map/pallas_call | solution.py:553
  37.0 5.5 %shard_map.96 = (f32[16,32,256]{2,1,0:T(8,128)}, f32[16,32,256]{2,1,0:T(8,128)}) custom-call(f32[22,48,256]{2,1,0:T(8,128)S(1)} %get-tuple-element.4.cond, f32[22,48,256]{2,1,0:T(8,128)S(1)} %get-tuple-element.5.start), custom_call_target="tpu_custom_call" | custom-call | tf_op jit(solution)/shard_map/pallas_call | solution.py:651

commit v4 on v3

--- a/solution.py
+++ b/solution.py
@@ -117,7 +117,7 @@
 
     @staticmethod
     def count(cuts, bands):
-        return 2 * len(bands) + 8 * len(cuts)
+        return 2 * len(bands) + 10 * len(cuts)
 
     def remote(self, src, dst, index, at):
         return pltpu.make_async_remote_copy(
@@ -135,13 +135,19 @@
             return self.nx + self.hx + c * size, size
         return self.hx - (c + 1) * size, size
 
-    def copy_x(self, d, c):
+    def copy_x(self, d, c, half=None):
         row, size = self.halo_rows(d, c)
         start = c * size if d == 0 else self.nx - (c + 1) * size
+        n = len(self.cuts)
+        if half is None:
+            col, cols, index = 0, self.ny, d * n + c
+        else:
+            col, cols = half * (self.ny // 2), self.ny // 2
+            index = (d if half == 0 else 8 + d) * n + half * 2 * len(self.bands) + c
         return self.remote(
-            self.brick(start, size, 0, self.ny),
-            self.ext.at[pl.ds(row, size), pl.ds(self.hy, self.ny)],
-            d * len(self.cuts) + c, self.at_x[d])
+            self.brick(start, size, col, cols),
+            self.ext.at[pl.ds(row, size), pl.ds(self.hy + col, cols)],
+            index, self.at_x[d])
 
     def copy_y(self, d, k):
         a, b = self.bands[k]
@@ -210,13 +216,13 @@
         self.each_mid(
             self.has_x[::-1], lambda side, d: self.copy_mid(side, d, c).wait_recv())
 
-    def start_x(self, c):
-        for d in range(2):
-            pl.when(self.has_x[d])(lambda d=d: self.copy_x(d, c).start())
-
-    def sent_x(self, c):
-        for d in range(2):
-            pl.when(self.has_x[d])(lambda d=d: self.copy_x(d, c).wait_send())
+    def start_x(self, c, half=None):
+        for d in range(2):
+            pl.when(self.has_x[d])(lambda d=d: self.copy_x(d, c, half).start())
+
+    def sent_x(self, c, half=None):
+        for d in range(2):
+            pl.when(self.has_x[d])(lambda d=d: self.copy_x(d, c, half).wait_send())
 
     def start_y(self, k):
         for d in range(2):
@@ -236,12 +242,12 @@
                 self.ext[:, pl.ds(at, self.hy)] = jnp.zeros((rows, self.hy, z), F32)
 
     def forward(self, c):
-        for side in range(2):
-            @pl.when(self.has_x[1 - side])
-            def _(side=side):
-                self.copy_x(side, c).wait_recv()
-                for d in range(2):
-                    pl.when(self.passes[d])(lambda d=d: self.copy_corner(side, d, c).start())
+        for d in range(2):
+            for side in range(2):
+                @pl.when(self.has_x[1 - side])
+                def _(side=side, d=d):
+                    self.copy_x(side, c, d).wait_recv()
+                    pl.when(self.passes[d])(lambda: self.copy_corner(side, d, c).start())
 
     def wait_y(self, k):
         for d in range(2):
@@ -259,10 +265,12 @@
         for d in range(2):
             for k in range(len(self.bands)):
                 pl.when(self.has_y[d])(lambda d=d, k=k: self.copy_y(d, k).wait_send())
-        self.sent_x(len(self.cuts) - 1)
         if self.mid is None:
+            self.sent_x(0)
             self.each_diagonal(self.has_x, self.has_y, lambda copy: copy.wait_send())
             return
+        for half in range(2):
+            self.sent_x(len(self.cuts) - 1, half)
         for c in range(len(self.cuts)):
             for side in range(2):
                 for d in range(2):
@@ -292,17 +300,12 @@
 
 
 STEP = 5
-BEFORE = 0.5
 IMG_CUTS = tuple((a, a + STEP) for a in range(0, IMG_X, STEP))
 POT_CUTS = ((0, POT_X),)
 
 
 def brick_bands(bx):
-    low = [0, POT_X, 2 * POT_X]
-    bands = []
-    for a, b in zip(low, low[1:]):
-        bands += [(a, b), (bx - b, bx - a)]
-    return tuple(bands) + ((low[-1], bx - low[-1]),)
+    return ((0, POT_X), (bx - POT_X, bx), (POT_X, bx - POT_X))
 
 
 def tensor_kernel(image, phases_in, table_in, start, wg_in, ws_in, zg_in, zs_in, cond, pot,
@@ -332,8 +335,9 @@
     for load in loads:
         load.start()
     greet()
-    img.start_x(0)
+    img.start_x(0, 0)
     img.start_y(0)
+    img.start_x(0, 1)
     own_start.start()
     for part in (img, pots, conds):
         part.clear()
@@ -403,7 +407,7 @@
 
     tiles_y, tiles_z = by // 8, z // 128
 
-    def smooth_x(known, ready, tiles, first=0, last=1):
+    def smooth_x(known, ready, tiles):
         new = [r in known and r not in ready for r in range(rows_x)]
 
         def tile(n):
@@ -428,23 +432,25 @@
         def step(n):
             for k in range(tiles):
                 tile(n * tiles + k)
-        count = 6 * tiles_y * tiles_z // tiles
-        begin, end = (round(count * part) for part in (first, last))
-        lax.fori_loop(begin, end, lambda n, carry: (step(n), carry)[1], 0)
+        loop(6 * tiles_y * tiles_z // tiles, step)
 
     along_z(IMG_X, bx, IMG_Y, by)
-    img.sent_x(0)
-    img.start_x(1)
+    img.sent_x(0, 0)
+    img.start_x(1, 0)
+    img.sent_x(0, 1)
+    img.start_x(1, 1)
     img.wait_y(0)
     img.start_mid(0)
     img.forward(0)
+    img.sent_x(1, 0)
+    img.start_x(2, 0)
     along_z(IMG_X, bx, 0, IMG_Y)
     along_z(IMG_X, bx, IMG_Y + by, IMG_Y)
-    img.sent_x(1)
-    img.start_x(2)
     img.start_mid(1)
+    img.sent_x(1, 1)
+    img.start_x(2, 1)
     img.start_mid(2)
-    core = range((chunks - 1) * STEP, rows_x - (chunks - 1) * STEP)
+    core = range(chunks * STEP, rows_x - chunks * STEP)
     inner = range(STEP, rows_x - STEP)
 
     def segment(part):
@@ -457,13 +463,12 @@
         @pl.when(part > 0)
         def _():
             c = part - 1
-            pl.when(part == chunks - 1)(lambda: smooth_x(core, (), 2, 0, BEFORE))
+            pl.when(part == 1)(lambda: smooth_x(core, (), 4))
             pl.when(part < chunks)(lambda: img.forward(c + 1))
 
             @pl.when(part == chunks - 1)
             def _():
                 pots.start_x(0)
-                smooth_x(core, (), 2, BEFORE, 1)
             img.wait_corner(c)
             along_z(bx + IMG_X + c * STEP, STEP, 0, wide_y)
             along_z(IMG_X - (c + 1) * STEP, STEP, 0, wide_y)
@@ -474,52 +479,61 @@
     for load in loads[3:]:
         load.wait()
 
-    def along_z_last(rows, slot):
+    def along_z_last(parts, slot):
         every = right(
-            jnp.concatenate([smooth[f, i] for i in rows for f in range(6)], axis=0),
+            jnp.concatenate([smooth[f, i, a:b] for i, a, b in parts for f in range(6)], axis=0),
             zs[:, :z], zs[:, z:])
-        grads[slot:slot + 6, :by] = every[:6 * by].reshape(6, by, z)
-        grads[slot:slot + 6, by:2 * by] = every[6 * by:].reshape(6, by, z)
-
-    def weigh(rows, slot):
-        for n, i in enumerate(rows):
+        at = 0
+        for n, (i, a, b) in enumerate(parts):
+            for f in range(6):
+                grads[slot + f, n * 16:n * 16 + b - a] = every[at:at + b - a]
+                at += b - a
+
+    def weigh(parts, slot):
+        for n, (i, a, b) in enumerate(parts):
             jxx, jyy, jzz, jxy, jxz, jyz = (
-                grads[slot + f, n * by:(n + 1) * by] for f in range(6))
+                grads[slot + f, n * 16:n * 16 + b - a] for f in range(6))
             trace = jxx + jyy + jzz
             shift = 0.1 * trace + 1e-06
-            a, b, c = jxx + shift, jyy + shift, jzz + shift
-            cof = a * b - jxy * jxy
+            p, q, c = jxx + shift, jyy + shift, jzz + shift
+            cof = p * q - jxy * jxy
             det = (
-                a * (b * c - jyz * jyz)
+                p * (q * c - jyz * jyz)
                 - jxy * (jxy * c - jyz * jxz)
-                + jxz * (jxy * jyz - b * jxz)
+                + jxz * (jxy * jyz - q * jxz)
             )
             weight = trace * cof / det
-            label = phases[i]
+            label = phases[i, a:b]
             base = jnp.where(
                 label == 0, table[0, 0], jnp.where(label == 1, table[0, 1], table[0, 2]))
             aniso = jnp.where(
                 label == 0, table[1, 0], jnp.where(label == 1, table[1, 1], table[1, 2]))
-            cond[POT_X + i, POT_Y:POT_Y + by] = base + 0.1 * aniso * weight
-
-    def rows_of(k):
-        return k, bx - 1 - k
-
-    pairs = bx // 2
-    for k in range(pairs + 1):
-        if k < pairs:
-            along_z_last(rows_of(k), 6 * (k % STEP))
+            cond[POT_X + i, POT_Y + a:POT_Y + b] = base + 0.1 * aniso * weight
+
+    outer = list(range(POT_X)) + list(range(bx - POT_X, bx))
+    rest = range(POT_X, bx - POT_X)
+    half = by // 2
+    units = [[(i, 0, half), (i, half, by)] for i in outer]
+    units = [units[k] + units[k + 1] for k in range(0, len(units), 2)]
+    first = len(units)
+    edges = [[(i, 0, POT_Y), (i, by - POT_Y, by)] for i in rest]
+    units += [edges[k] + edges[k + 1] for k in range(0, len(edges), 2)]
+    second = len(units)
+    middle = [[(i, POT_Y, by - POT_Y)] for i in rest]
+    units += [middle[k] + middle[k + 1] for k in range(0, len(middle), 2)]
+    for k in range(len(units) + 1):
+        if k < len(units):
+            along_z_last(units[k], 6 * (k % STEP))
         if k > 0:
-            weigh(rows_of(k - 1), 6 * ((k - 1) % STEP))
-        if k == POT_X:
+            weigh(units[k - 1], 6 * ((k - 1) % STEP))
+        if k == first:
             conds.start_x(0)
             conds.start_diagonal()
             conds.start_y(0)
             conds.start_y(1)
-        if k == 2 * POT_X:
+        if k == second:
             conds.start_y(2)
-            conds.start_y(3)
-    conds.start_y(4)
+
 
     own_start.wait()
     pots.wait_all()

time: 42.7 us -> 41.8 us (0.979); the launches traced: 42.4 us -> 41.1 us
  Pallas kernels: 41.8 us -> 40.4 us
    pallas_call x1, Pallas kernels: 36.3 us -> 35 us  [tensor(): pl.pallas_call(tensor_kernel, out_shape=[outer, outer], in_specs=[anywher...]
where the time goes in v4:
time: 41.8 us; the launch traced here: 41.1 us
  Pallas kernels  40.4 us (97%)
  between operations  0.64 us (2%)
    pallas_call x1, Pallas kernels, tensor(): pl.pallas_call(tensor_kernel, out_shape=[outer, outer], in_specs=[anywher...  35 us
    pallas_call x1, Pallas kernels, sweeps(): pl.pallas_call(sweep_kernel, out_shape=[brick, brick], in_specs=[vmem] *...  5.46 us

profile of v4, /device:TPU:3, one launch (start us, length us, event | category | flops | bytes accessed | tf_op | source)
XLA Modules:
  0.0 41.1 jit_solution(7346610878252975055)
XLA Ops:
  0.6 35.0 %shard_map.95 = (f32[22,48,256]{2,1,0:T(8,128)S(1)}, f32[22,48,256]{2,1,0:T(8,128)S(1)}) custom-call(f32[16,32,256]{2,1,0:T(8,128)} %image.1, s32[16,32,256]{2,1,0:T(8,128)} %phases_in.1, f32[2,3]{1,0:T(2,128)} %table_in.1, f32[16,32,256]{2,1,0:T(8,128)} %start.1, bf16[128,192]{1,0:T(8,128)(2,1)} %constant.8.clone.wg_in, ...), custom_call_target="tpu_custom_call" | custom-call | tf_op jit(solution)/shard_map/pallas_call | solution.py:567
  35.6 5.5 %shard_map.96 = (f32[16,32,256]{2,1,0:T(8,128)}, f32[16,32,256]{2,1,0:T(8,128)}) custom-call(f32[22,48,256]{2,1,0:T(8,128)S(1)} %get-tuple-element.4.cond, f32[22,48,256]{2,1,0:T(8,128)S(1)} %get-tuple-element.5.start), custom_call_target="tpu_custom_call" | custom-call | tf_op jit(solution)/shard_map/pallas_call | solution.py:665

commit v5 on v4

--- a/solution.py
+++ b/solution.py
@@ -19,6 +19,7 @@
 POT_X = SWEEPS
 POT_Y = 8
 MESH = pl.DeviceIdType.MESH
+PIECES = 4
 VMEM_LIMIT = 32 * 1024 * 1024
 F32 = jnp.float32
 BF16 = jnp.bfloat16
@@ -463,8 +464,8 @@
         @pl.when(part > 0)
         def _():
             c = part - 1
+            pl.when(part < chunks)(lambda: img.forward(c + 1))
             pl.when(part == 1)(lambda: smooth_x(core, (), 4))
-            pl.when(part < chunks)(lambda: img.forward(c + 1))
 
             @pl.when(part == chunks - 1)
             def _():
@@ -596,7 +597,7 @@
     return max(n for n in (1, 2, 3, 4) if count % n == 0)
 
 
-def sweep_kernel(cond, start, centre, out, kx, y0, y1, z0, z1, inv, one, two,
+def sweep_kernel(cond, start, centre, out, kx, y0, y1, z0, z1, inv, one, two, three,
                  *sems):
     rows, wide, z = cond.shape
     copy = pltpu.make_async_copy(
@@ -629,33 +630,49 @@
         y0[pl.ds(j, size)] = y_down
         y1[pl.ds(j, size)] = y_up
         z0[pl.ds(j, size)] = low
-        z1[pl.ds(j, size)] = high
+        z1[pl.ds(j, size)] = jnp.where(at_high, 0.0, z_up)
         inv[pl.ds(j, size)] = 1.0 / jnp.where(total > 0, total, 1.0)
         return carry
 
     lax.fori_loop(0, (rows - 2) // size, coefficients, 0)
 
-    def sweep(src, dst, shift, cols, first, last):
+    def relaxed(src, j, size, first, last):
+        at, cols = pl.ds(j, size), pl.ds(first, last - first)
+        p = src[at]
+        own = p[:, first:last]
+        if first > 0:
+            below, above = p[:, first - 1:last - 1], p[:, first + 1:last + 1]
+        else:
+            below, above = roll_y(p, 1), roll_y(p, -1)
+        numer = kx[pl.ds(j - 1, size), cols] * src[pl.ds(j - 1, size), cols]
+        numer = numer + kx[at, cols] * src[pl.ds(j + 1, size), cols]
+        numer = numer + y0[at, cols] * below + y1[at, cols] * above
+        numer = numer + z0[at, cols] * jnp.where(at_low[:, first:last], 1.0, roll_z(own, 1))
+        numer = numer + z1[at, cols] * roll_z(own, -1)
+        return numer * inv[at, cols]
+
+    def sweep(src, dst, first, last):
         size = step_of(last - first)
 
         def step(k, carry):
             j = first + k * size
-            at = pl.ds(j, size)
-            p = src[at]
-            numer = kx[pl.ds(j - 1, size)] * src[pl.ds(j - 1, size)]
-            numer = numer + kx[at] * src[pl.ds(j + 1, size)]
-            numer = numer + y0[at] * roll_y(p, 1) + y1[at] * roll_y(p, -1)
-            numer = numer + z0[at] * jnp.where(at_low, 1.0, roll_z(p, 1))
-            numer = numer + z1[at] * jnp.where(at_high, 0.0, roll_z(p, -1))
-            value = numer * inv[at]
-            dst[pl.ds(j - shift, size)] = value[:, cols:wide - cols]
+            dst[pl.ds(j, size)] = relaxed(src, j, size, 0, wide)
             return carry
         lax.fori_loop(0, (last - first) // size, step, 0)
 
-    sweep(start, one, 0, 0, 1, rows - 1)
-    sweep(one, two, 0, 0, 2, rows - 2)
-    sweep(two, out, POT_X, POT_Y, 3, rows - 3)
+    sweep(start, one, 1, rows - 1)
+    sweep(one, two, 2, rows - 2)
+    brick = rows - 2 * POT_X
+    size = brick // PIECES
+    sends = []
+    for k in range(PIECES):
+        part = pl.ds(k * size, size)
+        three[part] = relaxed(two, POT_X + k * size, size, POT_Y, wide - POT_Y)
+        sends.append(pltpu.make_async_copy(three.at[part], out.at[part], sems[1 + k]))
+        sends[-1].start()
     copy.wait()
+    for send in sends:
+        send.wait()
 
 
 def sweeps(cond_ext, pot_ext):
@@ -666,8 +683,9 @@
         sweep_kernel,
         out_shape=[brick, brick],
         in_specs=[vmem] * 2,
-        out_specs=[pl.BlockSpec(memory_space=pl.ANY), vmem],
-        scratch_shapes=[pltpu.VMEM((rows, wide, z), F32)] * 8 + [pltpu.SemaphoreType.DMA],
+        out_specs=[pl.BlockSpec(memory_space=pl.ANY)] * 2,
+        scratch_shapes=[pltpu.VMEM((rows, wide, z), F32)] * 8 + [
+            pltpu.VMEM(brick.shape, F32)] + [pltpu.SemaphoreType.DMA] * (1 + PIECES),
         compiler_params=pltpu.CompilerParams(vmem_limit_bytes=VMEM_LIMIT),
     )(cond_ext, pot_ext)
 

time: 41.8 us -> 40.3 us (0.964); the launches traced: 41.1 us -> 40 us
  Pallas kernels: 40.4 us -> 39.4 us
    pallas_call x1, Pallas kernels: 35 us -> 34.2 us  [tensor(): pl.pallas_call(tensor_kernel, out_shape=[outer, outer], in_specs=[anywher...]
where the time goes in v5:
time: 40.3 us; the launch traced here: 40 us
  Pallas kernels  39.4 us (98%)
  between operations  0.64 us (2%)
    pallas_call x1, Pallas kernels, tensor(): pl.pallas_call(tensor_kernel, out_shape=[outer, outer], in_specs=[anywher...  34.2 us
    pallas_call x1, Pallas kernels, sweeps(): pl.pallas_call(sweep_kernel, out_shape=[brick, brick], in_specs=[vmem] *...  5.18 us

profile of v5, /device:TPU:3, one launch (start us, length us, event | category | flops | bytes accessed | tf_op | source)
XLA Modules:
  0.0 40.0 jit_solution(7953127641876154791)
XLA Ops:
  0.6 34.2 %shard_map.95 = (f32[22,48,256]{2,1,0:T(8,128)S(1)}, f32[22,48,256]{2,1,0:T(8,128)S(1)}) custom-call(f32[16,32,256]{2,1,0:T(8,128)} %image.1, s32[16,32,256]{2,1,0:T(8,128)} %phases_in.1, f32[2,3]{1,0:T(2,128)} %table_in.1, f32[16,32,256]{2,1,0:T(8,128)} %start.1, bf16[128,192]{1,0:T(8,128)(2,1)} %constant.8.clone.wg_in, ...), custom_call_target="tpu_custom_call" | custom-call | tf_op jit(solution)/shard_map/pallas_call | solution.py:568
  34.9 5.2 %shard_map.96 = (f32[16,32,256]{2,1,0:T(8,128)}, f32[16,32,256]{2,1,0:T(8,128)}) custom-call(f32[22,48,256]{2,1,0:T(8,128)S(1)} %get-tuple-element.4.cond, f32[22,48,256]{2,1,0:T(8,128)S(1)} %get-tuple-element.5.start), custom_call_target="tpu_custom_call" | custom-call | tf_op jit(solution)/shard_map/pallas_call | solution.py:682

commit v6 on v5

--- a/solution.py
+++ b/solution.py
@@ -336,8 +336,8 @@
     for load in loads:
         load.start()
     greet()
+    img.start_y(0)
     img.start_x(0, 0)
-    img.start_y(0)
     img.start_x(0, 1)
     own_start.start()
     for part in (img, pots, conds):
@@ -445,9 +445,9 @@
     img.forward(0)
     img.sent_x(1, 0)
     img.start_x(2, 0)
+    img.start_mid(1)
     along_z(IMG_X, bx, 0, IMG_Y)
     along_z(IMG_X, bx, IMG_Y + by, IMG_Y)
-    img.start_mid(1)
     img.sent_x(1, 1)
     img.start_x(2, 1)
     img.start_mid(2)
@@ -457,6 +457,7 @@
     def segment(part):
         @pl.when(part == chunks)
         def _():
+            pots.start_x(0)
             pots.start_y(0)
             pots.start_diagonal()
             smooth_x(inner, core, 4)
@@ -465,11 +466,8 @@
         def _():
             c = part - 1
             pl.when(part < chunks)(lambda: img.forward(c + 1))
-            pl.when(part == 1)(lambda: smooth_x(core, (), 4))
-
-            @pl.when(part == chunks - 1)
-            def _():
-                pots.start_x(0)
+            pl.when(part == 1)(lambda: smooth_x(core, (), 2))
+
             img.wait_corner(c)
             along_z(bx + IMG_X + c * STEP, STEP, 0, wide_y)
             along_z(IMG_X - (c + 1) * STEP, STEP, 0, wide_y)

time: 40.3 us -> 40.3 us (level)
  no operation moved by 1% of the time
where the time goes in v6:
time: 40.3 us; the launch traced here: 40 us
  Pallas kernels  39.3 us (98%)
  between operations  0.64 us (2%)
    pallas_call x1, Pallas kernels, tensor(): pl.pallas_call(tensor_kernel, out_shape=[outer, outer], in_specs=[anywher...  34.2 us
    pallas_call x1, Pallas kernels, sweeps(): pl.pallas_call(sweep_kernel, out_shape=[brick, brick], in_specs=[vmem] *...  5.18 us

profile of v6, /device:TPU:3, one launch (start us, length us, event | category | flops | bytes accessed | tf_op | source)
XLA Modules:
  0.0 40.0 jit_solution(9648524620293990288)
XLA Ops:
  0.6 34.2 %shard_map.95 = (f32[22,48,256]{2,1,0:T(8,128)S(1)}, f32[22,48,256]{2,1,0:T(8,128)S(1)}) custom-call(f32[16,32,256]{2,1,0:T(8,128)} %image.1, s32[16,32,256]{2,1,0:T(8,128)} %phases_in.1, f32[2,3]{1,0:T(2,128)} %table_in.1, f32[16,32,256]{2,1,0:T(8,128)} %start.1, bf16[128,192]{1,0:T(8,128)(2,1)} %constant.8.clone.wg_in, ...), custom_call_target="tpu_custom_call" | custom-call | tf_op jit(solution)/shard_map/pallas_call | solution.py:566
  34.8 5.2 %shard_map.96 = (f32[16,32,256]{2,1,0:T(8,128)}, f32[16,32,256]{2,1,0:T(8,128)}) custom-call(f32[22,48,256]{2,1,0:T(8,128)S(1)} %get-tuple-element.4.cond, f32[22,48,256]{2,1,0:T(8,128)S(1)} %get-tuple-element.5.start), custom_call_target="tpu_custom_call" | custom-call | tf_op jit(solution)/shard_map/pallas_call | solution.py:680
